TPU v7x, 128 devices: a whole 4x4x4 slice. The times are simulated.
128 devices in a mesh: ctx: 32 (over z, y, core), tp: 4 (over x).
Axes of the slice: x: 4, y: 4, z: 4, core: 2. Of those that a mesh axis runs over, the one named last changes fastest.
Arguments:
- x_tokens: bfloat16 [16384, 4096], P('ctx', 'tp'), may hold values from -60 to 60
- w_query: bfloat16 [4096, 4096], P(None, 'tp'), may hold values from -0.09375 to 0.09375
- w_key: bfloat16 [4096, 1024], P(None, 'tp'), may hold values from -0.09375 to 0.09375
- w_value: bfloat16 [4096, 1024], P(None, 'tp'), may hold values from -0.09375 to 0.09375
- w_output: bfloat16 [4096, 4096], P('tp'), may hold values from -0.09375 to 0.09375
- pattern: int32 [128, 8], P('ctx'), may hold values from 0 to 127, as said below
- doc_lengths: int32 [16], replicated, may hold values from 1 to 10240, 16384 in all
Outputs:
- attn_out: bfloat16 [16384, 4096], P(('ctx', 'tp'))
Inputs may be any that keep to these rules, and one draw needn't show every extreme that they name: `pattern`: row q has 8 entries; the first is q itself and every entry is at most q; entries may repeat. The rows of one index of ctx (4 rows) name at most 2 distinct blocks held by any other index of ctx (index i holding blocks i * 4 onward), and exactly 2 of index 0 for every other index. Every row of an index i in the upper half of ctx names 2 blocks of index i minus half the number of ctx indices.
All inputs are finite; a program needn't handle non-finite values.
Results may differ from a plain program's by a relative error of at most 0.02.
Values may be sent and summed in bfloat16 or wider, within the bound.
No kernel may reach another device: no remote copies, remote signals or barrier semaphores. Data moves between devices by JAX's collectives and lax.ppermute only.
A program may use at most 128 MiB of HBM per device.

v0:
```python
import jax
import jax.numpy as jnp
from jax import lax
from jax.sharding import PartitionSpec as P

HD = 128
BLK = 128
LIST = 8
ROPE_BASE = 500000.0
NEG_LARGE = -1e30


def rotate(projected, head_count, positions):
    split_heads = projected.reshape(projected.shape[0], head_count, HD)
    frequency = ROPE_BASE ** (-(jnp.arange(HD // 2, dtype=jnp.float32) * 2.0 / HD))
    angles = positions.astype(jnp.float32)[:, None] * frequency[None, :]
    cosine_table = jnp.cos(angles)[:, None, :]
    sine_table = jnp.sin(angles)[:, None, :]
    front_half = split_heads[..., : HD // 2]
    back_half = split_heads[..., HD // 2 :]
    return jnp.concatenate(
        [
            front_half * cosine_table - back_half * sine_table,
            back_half * cosine_table + front_half * sine_table,
        ],
        axis=-1,
    )


def document_of(positions, doc_lengths):
    ends = jnp.cumsum(doc_lengths)
    return jnp.sum((ends[None, :] <= positions[:, None]).astype(jnp.int32), axis=1)


def fresh_entries(pattern):
    equal = pattern[:, :, None] == pattern[:, None, :]
    earlier = jnp.tril(jnp.ones((LIST, LIST), dtype=bool), -1)
    return jnp.logical_not(jnp.any(equal & earlier[None], axis=2))


def attend_listed(
    query,
    chosen_keys,
    chosen_values,
    pattern,
    positions,
    documents,
    doc_lengths,
    kv_heads,
    group_size,
):
    local_rows = positions.shape[0]
    block_count = local_rows // BLK
    fresh = fresh_entries(pattern)
    offsets_in = jnp.arange(BLK, dtype=jnp.int32)
    key_index = (pattern[:, :, None] * BLK + offsets_in[None, None, :]).reshape(
        block_count, LIST * BLK
    )
    key_ok = jnp.repeat(fresh, BLK, axis=1)
    key_doc = document_of(key_index.reshape(-1), doc_lengths).reshape(key_index.shape)
    block_pos = positions.reshape(block_count, BLK)
    block_doc = documents.reshape(block_count, BLK)
    block_query = query.reshape(block_count, BLK, kv_heads, group_size, HD)
    allowed = (
        (key_index[:, None, :] <= block_pos[:, :, None])
        & (key_doc[:, None, :] == block_doc[:, :, None])
        & key_ok[:, None, :]
    )
    allowed = allowed[:, None, None, :, :]
    scores = jnp.einsum(
        "bqkgd,blkd->bkgql", block_query, chosen_keys, preferred_element_type=jnp.float32
    )
    masked = jnp.where(allowed, scores, NEG_LARGE)
    row_max = jnp.max(masked, axis=-1, keepdims=True)
    weights = jnp.where(allowed, jnp.exp(masked - row_max), 0.0)
    total = jnp.sum(weights, axis=-1)
    mixed = jnp.einsum(
        "bkgql,blkd->bkgqd",
        weights.astype(jnp.bfloat16),
        chosen_values,
        preferred_element_type=jnp.float32,
    )
    mixed = mixed / total[..., None]
    return (
        jnp.transpose(mixed, (0, 3, 1, 2, 4))
        .reshape(local_rows, kv_heads * group_size * HD)
        .astype(jnp.bfloat16)
    )


def on_device(x_tokens, w_query, w_key, w_value, w_output, pattern, doc_lengths):
    features = lax.all_gather(x_tokens, "tp", axis=1, tiled=True)
    local_rows = features.shape[0]
    query_heads = w_query.shape[1] // HD
    kv_heads = w_key.shape[1] // HD
    group_size = query_heads // kv_heads
    block_count = local_rows // BLK
    positions = lax.axis_index("ctx") * local_rows + jnp.arange(local_rows, dtype=jnp.int32)
    query = rotate(
        jnp.dot(features, w_query, preferred_element_type=jnp.float32), query_heads, positions
    ) * HD ** (-0.5)
    query = query.astype(jnp.bfloat16).reshape(local_rows, kv_heads, group_size, HD)
    keys = rotate(jnp.dot(features, w_key, preferred_element_type=jnp.float32), kv_heads, positions)
    keys = keys.astype(jnp.bfloat16).reshape(local_rows, kv_heads * HD)
    values = jnp.dot(features, w_value, preferred_element_type=jnp.float32).astype(jnp.bfloat16)
    documents = document_of(positions, doc_lengths)
    every_key, every_value = (
        lax.all_gather(keys, "ctx", axis=0, tiled=True),
        lax.all_gather(values, "ctx", axis=0, tiled=True),
    )
    offsets_in = jnp.arange(BLK, dtype=jnp.int32)
    key_index = (pattern[:, :, None] * BLK + offsets_in[None, None, :]).reshape(
        block_count, LIST * BLK
    )
    chosen_keys = every_key[key_index].reshape(block_count, LIST * BLK, kv_heads, HD)
    chosen_values = every_value[key_index].reshape(block_count, LIST * BLK, kv_heads, HD)
    attended = attend_listed(
        query,
        chosen_keys,
        chosen_values,
        pattern,
        positions,
        documents,
        doc_lengths,
        kv_heads,
        group_size,
    )
    return lax.psum_scatter(
        jnp.dot(attended, w_output, preferred_element_type=jnp.float32).astype(jnp.bfloat16),
        "tp",
        scatter_dimension=0,
        tiled=True,
    )


def solution(mesh):
    return jax.shard_map(
        on_device,
        mesh=mesh,
        in_specs=(
            P("ctx", "tp"),
            P(None, "tp"),
            P(None, "tp"),
            P(None, "tp"),
            P("tp", None),
            P("ctx", None),
            P(),
        ),
        out_specs=P(("ctx", "tp"), None),
        check_vma=False,
    )
```

profile of v0, /device:TPU:1, one launch (start us, length us, event | category | flops | bytes accessed | tf_op | source)
XLA Modules:
  0.0 297.7 jit_solution(13942825732113829720)
XLA Ops:
  6.5 0.7 all-gather.4.cloned.1.call-update
  7.3 53.2 %all-gather.4.cloned.1.call-done = bf16[512,4096]{1,0:T(8,128)(2,1)} async-done(((bf16[512,1024]{1,0:T(8,128)(2,1)}), bf16[512,4096]{1,0:T(8,128)(2,1)}) %all-gather.4.cloned.1.call-update) | async-done | bytes 4194320 | tf_op jit(solution)/shard_map/all_gather | solution.py:92
  60.5 4.1 %convolution_convert_fusion.1 = bf16[512,256]{1,0:T(8,128)(2,1)} fusion(bf16[512,4096]{1,0:T(8,128)(2,1)} %all-gather.4.cloned.1.call-done, bf16[4096,256]{1,0:T(8,128)(2,1)S(1)} %copy-done), kind=kOutput, calls=%fused_computation.19 | convolution fusion | flops 1073872896 | bytes 6553600 | tf_op jit(solution)/shard_map/dot_general | solution.py:105
  65.2 4.2 %fusion.23 = f32[512,256]{0,1:T(8,128)S(1)} fusion(bf16[512,4096]{1,0:T(8,128)(2,1)} %all-gather.4.cloned.1.call-done, bf16[4096,256]{1,0:T(8,128)(2,1)} %param.9), kind=kOutput, calls=%fused_computation.51 | convolution fusion | flops 1073741824 | bytes 6815744 | tf_op jit(solution)/shard_map/dot_general | solution.py:103
  69.6 0.9 copy.38
  71.8 3.9 %and_and_fusion = pred[4,128,1024]{1,2,0:T(8,128)(4,1)} fusion(s32[4,128]{1,0:T(4,128)S(1)} %bitcast.60, s32[4,1024]{1,0:T(4,128)S(1)} %eq.34, s32[4,128]{1,0:T(4,128)S(1)} %add_add_fusion, s32[4,1024]{1,0:T(4,128)S(1)} %bitcast_add_fusion, pred[4,1024]{1,0:T(4,128)(4,1)S(1)} %bitcast.59), kind=kLoop, calls=%fused_computation.18 | loop fusion | flops 2097152 | bytes 565248 | tf_op jit(solution)/shard_map/and | solution.py:65
  75.7 8.3 %fusion.24 = f32[512,1024]{0,1:T(8,128)S(1)} fusion(bf16[512,4096]{1,0:T(8,128)(2,1)} %all-gather.4.cloned.1.call-done, bf16[4096,1024]{1,0:T(8,128)(2,1)} %param.8), kind=kOutput, calls=%fused_computation.52 | convolution fusion | flops 4294967296 | bytes 14680064 | tf_op jit(solution)/shard_map/reshape | solution.py:14
  84.3 1.3 concatenate.13
  85.6 1.7 copy.29
  87.4 1.3 concatenate.14
  88.7 2.7 copy.30
  91.4 27.2 %all-gather.8.cloned.1.call-done = bf16[16384,256]{1,0:T(8,128)(2,1)} async-done(((bf16[512,256]{1,0:T(8,128)(2,1)}), bf16[16384,256]{1,0:T(8,128)(2,1)}) %all-gather.8.cloned.1.call-update) | async-done | bytes 8388624 | tf_op jit(solution)/shard_map/all_gather | solution.py:109
  118.6 20.4 %gather_fusion.1 = bf16[4096,256]{1,0:T(8,128)(2,1)} fusion(bf16[16384,256]{1,0:T(8,128)(2,1)} %all-gather.8.cloned.1.call-done, s32[4096]{0:T(1024)S(1)} %bitcast_clamp_fusion), kind=kCustom, calls=%fused_computation.1 | custom fusion | bytes 4210688 | tf_op jit(solution)/shard_map/gather | solution.py:116
  139.0 4.0 %reshape.220 = bf16[4,1024,2,128]{3,2,1,0:T(2,128)(2,1)} reshape(bf16[4096,256]{1,0:T(8,128)(2,1)} %gather_fusion.1) | data formatting | bytes 4194304 | tf_op jit(solution)/shard_map/reshape | solution.py:116
  143.0 30.5 %all-gather.6.cloned.1.call-done = bf16[16384,256]{1,0:T(8,128)(2,1)} async-done(((bf16[512,256]{1,0:T(8,128)(2,1)}), bf16[16384,256]{1,0:T(8,128)(2,1)}) %all-gather.6.cloned.1.call-update) | async-done | bytes 8388624 | tf_op jit(solution)/shard_map/all_gather | solution.py:108
  173.4 20.4 %gather_fusion = bf16[4096,256]{1,0:T(8,128)(2,1)} fusion(bf16[16384,256]{1,0:T(8,128)(2,1)} %all-gather.6.cloned.1.call-done, s32[4096]{0:T(1024)S(1)} %bitcast_clamp_fusion), kind=kCustom, calls=%fused_computation | custom fusion | bytes 4210688 | tf_op jit(solution)/shard_map/gather | solution.py:115
  193.8 4.0 %reshape.218 = bf16[4,1024,2,128]{3,2,1,0:T(2,128)(2,1)} reshape(bf16[4096,256]{1,0:T(8,128)(2,1)} %gather_fusion) | data formatting | bytes 4194304 | tf_op jit(solution)/shard_map/reshape | solution.py:115
  197.8 10.5 %fusion.9 = f32[4,2,1024,128,4]{3,2,4,1,0:T(8,128)} fusion(bf16[4,1024,2,128,1]{3,2,1,0,4:T(2,128)(2,1)} %bitcast.54, f32[4,128,2,4,64]{4,1,3,2,0:T(8,128)} %copy.30, f32[4,128,2,4,64]{4,1,3,2,0:T(8,128)S(1)} %copy.29), kind=kOutput, calls=%fused_computation.16 | convolution fusion | flops 1075314688 | bytes 20971520 | tf_op jit(solution)/shard_map/bqkgd,blkd->bkgql/dot_general | solution.py:70
  208.3 19.6 %fusion.22 = (f32[4,2,4,128]{3,2,1,0:T(4,128)S(1)}, bf16[4,2,4,128,1024]{3,4,2,1,0:T(8,128)(2,1)}) fusion(f32[4,2,1024,128,4]{3,2,4,1,0:T(8,128)} %fusion.9, pred[4,128,1024]{1,2,0:T(8,128)(4,1)S(1)} %copy-done.3), kind=kOutput, calls=%fused_computation.50 | output fusion | flops 25166848 | bytes 25706496 | tf_op jit(solution)/shard_map/sub | solution.py:75
  227.9 6.2 %fusion.7 = bf16[4,128,2,4,128]{4,1,3,2,0:T(8,128)(2,1)S(1)} fusion(f32[4,128,2,4]{1,3,2,0:T(4,128)S(1)} %bitcast.62, bf16[4,1024,2,128,1]{3,2,1,0,4:T(2,128)(2,1)S(1)} %bitcast.55, bf16[4,2,4,128,1024]{3,4,2,1,0:T(8,128)(2,1)} %get-tuple-element.14), kind=kOutput, calls=%fused_computation.14 | convolution fusion | flops 1074790400 | bytes 11550720 | tf_op jit(solution)/shard_map/bkgql,blkd->bkgqd/dot_general | solution.py:77
  234.1 0.8 copy.34
  234.9 0.8 convert_element_type.46
  235.7 9.4 %convolution_convert_fusion = bf16[512,4096]{1,0:T(8,128)(2,1)} fusion(bf16[512,1024]{1,0:T(8,128)(2,1)S(1)} %convert_element_type.46, bf16[1024,4096]{1,0:T(8,128)(2,1)} %param.11), kind=kOutput, calls=%fused_computation.10 | convolution fusion | flops 4297064448 | bytes 13631488 | tf_op jit(solution)/shard_map/dot_general | solution.py:129
  245.1 46.0 %reduce-scatter.2.cloned.1.call-done = bf16[128,4096]{1,0:T(8,128)(2,1)} async-done(((bf16[512,4096]{1,0:T(8,128)(2,1)}), bf16[128,4096]{1,0:T(8,128)(2,1)}) %reduce-scatter.2.cloned.1.call-update) | async-done | bytes 1048592 | tf_op jit(solution)/shard_map/reduce_scatter | solution.py:128
  (46 shorter events, 2.4 us)
Async XLA Ops:
  6.5 53.9 %copy-start = (bf16[4096,256]{1,0:T(8,128)(2,1)S(1)}, bf16[4096,256]{1,0:T(8,128)(2,1)}, u32[]{:S(2)}) copy-start(bf16[4096,256]{1,0:T(8,128)(2,1)} %param.10) | copy-start | bytes 6291460
  6.5 53.9 %all-gather.4.cloned.1.call-start = ((), (), s32[]{:S(2)}) async-start(), calls=%async_computation.1 | async-start | bytes 5242880 | tf_op jit(solution)/shard_map/all_gather | solution.py:92
  7.3 111.4 %all-gather.8.cloned.1.call-start = ((), (), s32[]{:S(2)}) async-start(), calls=%async_computation.3 | async-start | bytes 8650752 | tf_op jit(solution)/shard_map/all_gather | solution.py:109
  64.6 108.8 %all-gather.6.cloned.1.call-start = ((), (), s32[]{:S(2)}) async-start(), calls=%async_computation.2 | async-start | bytes 8650752 | tf_op jit(solution)/shard_map/all_gather | solution.py:108
  69.4 1.4 copy-start.4
  69.4 1.7 copy-start.5
  70.4 220.7 %reduce-scatter.2.cloned.1.call-start = ((), (), s32[]{:S(2)}) async-start(), calls=%async_computation.4 | async-start | bytes 5242880 | tf_op jit(solution)/shard_map/reduce_scatter | solution.py:128
  197.8 10.5 %copy-start.3 = (pred[4,128,1024]{1,2,0:T(8,128)(4,1)S(1)}, pred[4,128,1024]{1,2,0:T(8,128)(4,1)}, u32[]{:S(2)}) copy-start(pred[4,128,1024]{1,2,0:T(8,128)(4,1)} %and_and_fusion) | copy-start | bytes 1572868
  208.3 19.6 %copy-start.2 = (bf16[4,1024,2,128]{3,2,1,0:T(2,128)(2,1)S(1)}, bf16[4,1024,2,128]{3,2,1,0:T(2,128)(2,1)}, u32[]{:S(2)}) copy-start(bf16[4,1024,2,128]{3,2,1,0:T(2,128)(2,1)} %reshape.220) | copy-start | bytes 6291460
  245.1 46.1 %copy-start.1 = (bf16[4096,256]{1,0:T(8,128)(2,1)S(1)}, bf16[4096,256]{1,0:T(8,128)(2,1)}, u32[]{:S(2)}) copy-start(bf16[4096,256]{1,0:T(8,128)(2,1)} %param.10) | copy-start | bytes 6291460
Sparse Core Ops, SparseCore 0:
  9.0 51.3 all-gather.3
  64.7 53.8 all-gather.7
  120.9 52.5 all-gather.5
  245.2 45.8 reduce-scatter.1
where the time goes:
time: 298 us
  waiting for transfers between devices  158 us (53%)
  local copies, waits for them, and re-layouts  58.6 us (20%)
  matrix products  42.6 us (14%)
  other arithmetic  25.3 us (8%)
  between operations  13.3 us (4%)
    all_gather x1, waiting for transfers between devices, on_device(): features = lax.all_gather(x_tokens, 'tp', axis=1, tiled=True)  53.2 us
    reduce_scatter x1, waiting for transfers between devices, on_device(): lax.psum_scatter(jnp.dot(attended, w_output, preferred_element_type=jnp.f...  46 us
    all_gather x1, waiting for transfers between devices, on_device(): lax.all_gather(keys, 'ctx', axis=0, tiled=True)  30.5 us
    all_gather x1, waiting for transfers between devices, on_device(): lax.all_gather(values, 'ctx', axis=0, tiled=True)  27.2 us
    gather x1, local copies, waits for them, and re-layouts, on_device(): every_key[key_index].reshape(block_count, LIST * BLK, kv_heads, HD)  20.4 us
    gather x1, local copies, waits for them, and re-layouts, on_device(): every_value[key_index].reshape(block_count, LIST * BLK, kv_heads, HD)  20.4 us
    sub x1, other arithmetic, attend_listed(): weights = jnp.where(allowed, jnp.exp(masked - row_max), 0.0)  19.6 us
    dot_general x1, matrix products, attend_listed(): jnp.einsum('bqkgd,blkd->bkgql', block_query, chosen_keys, preferred_eleme...  10.5 us
  transfers between devices with their start and end apart: 4, of which 4 were waited for; matrix products, arithmetic and copies ran while one was open for 17% of the time, Pallas kernels for 0%

commit v1 on v0

--- a/solution.py
+++ b/solution.py
@@ -1,3 +1,4 @@
+import functools
 import jax
 import jax.numpy as jnp
 from jax import lax
@@ -8,6 +9,21 @@
 LIST = 8
 ROPE_BASE = 500000.0
 NEG_LARGE = -1e30
+
+
+def shifts_all_drive(content, which_dim):
+    t1, low, latest = (lax.axis_size("ctx"), lax.axis_index("ctx"), content.shape[which_dim])
+    value_now, reached = (content, 1)
+    while reached < t1:
+        pile = []
+        for c in range(t1):
+            pile.append((c, (c - reached) % t1))
+        value_now = jnp.concatenate([value_now, lax.ppermute(value_now, "ctx", pile)], which_dim)
+        reached = 2 * reached
+    return jnp.roll(value_now, low * latest, which_dim)
+
+
+save_loops_here = functools.partial(shifts_all_drive, which_dim=0)
 
 
 def rotate(projected, head_count, positions):
@@ -106,7 +122,7 @@
     documents = document_of(positions, doc_lengths)
     every_key, every_value = (
         lax.all_gather(keys, "ctx", axis=0, tiled=True),
-        lax.all_gather(values, "ctx", axis=0, tiled=True),
+        save_loops_here(values),
     )
     offsets_in = jnp.arange(BLK, dtype=jnp.int32)
     key_index = (pattern[:, :, None] * BLK + offsets_in[None, None, :]).reshape(

time: 298 us -> 449 us (1.51)
  waiting for transfers between devices: 158 us -> 268 us
  local copies, waits for them, and re-layouts: 58.6 us -> 83.9 us
  starting transfers between devices: 0.31 us -> 13.6 us
    ppermute x0 -> x5, waiting for transfers between devices: none -> 167 us  [shifts_all_drive(): lax.ppermute(value_now, 'ctx', pile)]
    all_gather x1, waiting for transfers between devices: 30.5 us -> 0.01 us  [on_device(): lax.all_gather(keys, 'ctx', axis=0, tiled=True)]
    all_gather x1 -> x0, waiting for transfers between devices: 27.2 us -> none  [on_device(): lax.all_gather(values, 'ctx', axis=0, tiled=True)]
    unnamed x14 -> x33, local copies, waits for them, and re-layouts: 0.11 us -> 14.2 us
    ppermute x0 -> x5, starting transfers between devices: none -> 13.5 us  [shifts_all_drive(): lax.ppermute(value_now, 'ctx', pile)]
    dynamic_slice x0 -> x1, local copies, waits for them, and re-layouts: none -> 7.02 us  [shifts_all_drive(): return jnp.roll(value_now, low * latest, which_dim)]
    concatenate x0 -> x2, local copies, waits for them, and re-layouts: none -> 6.75 us  [the longest x1 4.38 us: shifts_all_drive(): return jnp.roll(value_now, low * latest, which_dim)]
  transfers between devices with their start and end apart: 4 -> 8, of which waited for: 4 -> 7; matrix products, arithmetic and copies ran while one was open for 17% -> 17% of each run, Pallas kernels for 0% -> 0%
where the time goes in v1:
time: 449 us
  waiting for transfers between devices  268 us (60%)
  local copies, waits for them, and re-layouts  83.9 us (19%)
  matrix products  42.9 us (10%)
  other arithmetic  26.6 us (6%)
  starting transfers between devices  13.6 us (3%)
  between operations  13.3 us (3%)
    ppermute x5, waiting for transfers between devices, shifts_all_drive(): lax.ppermute(value_now, 'ctx', pile)  167 us
    all_gather x1, waiting for transfers between devices, on_device(): features = lax.all_gather(x_tokens, 'tp', axis=1, tiled=True)  52.6 us
    reduce_scatter x1, waiting for transfers between devices, on_device(): lax.psum_scatter(jnp.dot(attended, w_output, preferred_element_type=jnp.f...  48.4 us
    gather x1, local copies, waits for them, and re-layouts, on_device(): every_key[key_index].reshape(block_count, LIST * BLK, kv_heads, HD)  20.4 us
    sub x1, other arithmetic, attend_listed(): weights = jnp.where(allowed, jnp.exp(masked - row_max), 0.0)  19.8 us
    gather x1, local copies, waits for them, and re-layouts, on_device(): every_value[key_index].reshape(block_count, LIST * BLK, kv_heads, HD)  17.4 us
    unnamed x33, local copies, waits for them, and re-layouts  14.2 us
    ppermute x5, starting transfers between devices, shifts_all_drive(): lax.ppermute(value_now, 'ctx', pile)  13.5 us
  transfers between devices with their start and end apart: 8, of which 7 were waited for; matrix products, arithmetic and copies ran while one was open for 17% of the time, Pallas kernels for 0%

profile of v1, /device:TPU:1, one launch (start us, length us, event | category | flops | bytes accessed | tf_op | source)
XLA Modules:
  0.0 448.6 jit_solution(16691209694195011422)
XLA Ops:
  7.9 52.6 %all-gather.3.cloned.1.call-done = bf16[512,4096]{1,0:T(8,128)(2,1)} async-done(((bf16[512,1024]{1,0:T(8,128)(2,1)}), bf16[512,4096]{1,0:T(8,128)(2,1)}) %all-gather.3.cloned.1.call-update) | async-done | bytes 4194320 | tf_op jit(solution)/shard_map/all_gather | solution.py:108
  60.5 4.2 fusion.23
  65.7 4.2 constant_dynamic-update-slice_fusion.4
  70.6 5.1 %collective-permute-done = bf16[512,256]{1,0:T(8,128)(2,1)S(1)} collective-permute-done((bf16[512,256]{1,0:T(8,128)(2,1)S(1)}, bf16[512,256]{1,0:T(8,128)(2,1)S(1)}, u32[]{:S(2)}, u32[]{:S(2)}) %collective-permute-start) | collective-permute-done | bytes 262176 | tf_op jit(solution)/shard_map/ppermute | solution.py:21
  75.8 9.7 %collective-permute-start.1 = (bf16[1024,256]{1,0:T(8,128)(2,1)S(1)}, bf16[1024,256]{1,0:T(8,128)(2,1)S(1)}, u32[]{:S(2)}, u32[]{:S(2)}) collective-permute-start(bf16[1024,256]{1,0:T(8,128)(2,1)S(1)} %pad_maximum_fusion.2), channel_id=1, source_target_pairs={{0,120},{4,124},{8,0},{12,4},{16,8},{20,12},{24,16},{28,20},{32,24... | collective-permute-start | bytes 1572872 | tf_op jit(solution)/shard_map/ppermute | solution.py:21
  85.5 9.6 %collective-permute-done.1 = bf16[1024,256]{1,0:T(8,128)(2,1)S(1)} collective-permute-done((bf16[1024,256]{1,0:T(8,128)(2,1)S(1)}, bf16[1024,256]{1,0:T(8,128)(2,1)S(1)}, u32[]{:S(2)}, u32[]{:S(2)}) %collective-permute-start.1) | collective-permute-done | bytes 524320 | tf_op jit(solution)/shard_map/ppermute | solution.py:21
  95.2 3.0 collective-permute-start.2
  98.2 38.4 %collective-permute-done.2 = bf16[2048,256]{1,0:T(8,128)(2,1)S(1)} collective-permute-done((bf16[2048,256]{1,0:T(8,128)(2,1)S(1)}, bf16[2048,256]{1,0:T(8,128)(2,1)S(1)}, u32[]{:S(2)}, u32[]{:S(2)}) %collective-permute-start.2) | collective-permute-done | bytes 1048608 | tf_op jit(solution)/shard_map/ppermute | solution.py:21
  140.3 43.2 %collective-permute-done.3 = bf16[4096,256]{1,0:T(8,128)(2,1)S(1)} collective-permute-done((bf16[4096,256]{1,0:T(8,128)(2,1)S(1)}, bf16[4096,256]{1,0:T(8,128)(2,1)S(1)}, u32[]{:S(2)}, u32[]{:S(2)}) %collective-permute-start.3) | collective-permute-done | bytes 2097184 | tf_op jit(solution)/shard_map/ppermute | solution.py:21
  188.4 3.9 and_and_fusion
  192.3 8.3 %fusion.24 = f32[512,1024]{0,1:T(8,128)S(1)} fusion(bf16[512,4096]{1,0:T(8,128)(2,1)} %all-gather.3.cloned.1.call-done, bf16[4096,1024]{1,0:T(8,128)(2,1)} %param.8), kind=kOutput, calls=%fused_computation.73 | convolution fusion | flops 4294967296 | bytes 14680064 | tf_op jit(solution)/shard_map/reshape | solution.py:30
  204.4 2.7 copy.29
  211.1 70.1 %collective-permute-done.4 = bf16[8192,256]{1,0:T(8,128)(2,1)} collective-permute-done((bf16[8192,256]{1,0:T(8,128)(2,1)}, bf16[8192,256]{1,0:T(8,128)(2,1)}, u32[]{:S(2)}, u32[]{:S(2)}) %collective-permute-start.4) | collective-permute-done | bytes 4194336 | tf_op jit(solution)/shard_map/ppermute | solution.py:21
  281.3 4.4 constant_dynamic-update-slice_fusion.11
  290.6 4.4 constant_dynamic-update-slice_fusion.5
  294.9 7.0 %constant_dynamic-slice_fusion = bf16[16384,256]{1,0:T(8,128)(2,1)} fusion(bf16[32768,256]{1,0:T(8,128)(2,1)} %constant_dynamic-update-slice_fusion.5, s32[]{:T(128)S(6)} %select_n.37), kind=kLoop, calls=%fused_computation.68 | loop fusion | bytes 16777220 | tf_op jit(solution)/shard_map/jit(_roll_dynamic)/dynamic_slice | solution.py:23
  302.0 17.4 %gather_fusion.1 = bf16[4096,256]{1,0:T(8,128)(2,1)S(1)} fusion(bf16[16384,256]{1,0:T(8,128)(2,1)} %constant_dynamic-slice_fusion, s32[4096]{0:T(1024)S(1)} %bitcast_clamp_fusion), kind=kCustom, calls=%fused_computation.1 | custom fusion | bytes 4210688 | tf_op jit(solution)/shard_map/gather | solution.py:132
  321.6 20.4 %gather_fusion = bf16[4096,256]{1,0:T(8,128)(2,1)} fusion(bf16[16384,256]{1,0:T(8,128)(2,1)} %all-gather.5.cloned.1.call-done, s32[4096]{0:T(1024)S(1)} %bitcast_clamp_fusion), kind=kCustom, calls=%fused_computation | custom fusion | bytes 4210688 | tf_op jit(solution)/shard_map/gather | solution.py:131
  341.9 4.1 reshape.218
  346.1 10.5 %fusion.9 = f32[4,2,1024,128,4]{3,2,4,1,0:T(8,128)} fusion(bf16[4,1024,2,128,1]{3,2,1,0,4:T(2,128)(2,1)} %bitcast.54, f32[4,128,2,4,64]{4,1,3,2,0:T(8,128)} %copy.30, f32[4,128,2,4,64]{4,1,3,2,0:T(8,128)S(1)} %copy-done.4), kind=kOutput, calls=%fused_computation.17 | convolution fusion | flops 1075314688 | bytes 20971520 | tf_op jit(solution)/shard_map/bqkgd,blkd->bkgql/dot_general | solution.py:86
  356.6 19.8 %fusion.22 = (f32[4,2,4,128]{3,2,1,0:T(4,128)S(1)}, bf16[4,2,4,128,1024]{3,4,2,1,0:T(8,128)(2,1)}) fusion(f32[4,2,1024,128,4]{3,2,4,1,0:T(8,128)} %fusion.9, pred[4,128,1024]{1,2,0:T(8,128)(4,1)S(1)} %copy-done.8), kind=kOutput, calls=%fused_computation.71 | output fusion | flops 25166848 | bytes 25706496 | tf_op jit(solution)/shard_map/sub | solution.py:91
  376.3 6.2 %fusion.7 = bf16[4,128,2,4,128]{4,1,3,2,0:T(8,128)(2,1)S(1)} fusion(f32[4,128,2,4]{1,3,2,0:T(4,128)S(1)} %bitcast.62, bf16[4,1024,2,128,1]{3,2,1,0,4:T(2,128)(2,1)S(1)} %bitcast.55, bf16[4,2,4,128,1024]{3,4,2,1,0:T(8,128)(2,1)} %get-tuple-element.24), kind=kOutput, calls=%fused_computation.15 | convolution fusion | flops 1074790400 | bytes 11550720 | tf_op jit(solution)/shard_map/bkgql,blkd->bkgqd/dot_general | solution.py:93
  384.1 9.5 %convolution_convert_fusion = bf16[512,4096]{1,0:T(8,128)(2,1)} fusion(bf16[512,1024]{1,0:T(8,128)(2,1)S(1)} %convert_element_type.46, bf16[1024,4096]{1,0:T(8,128)(2,1)} %param.11), kind=kOutput, calls=%fused_computation.10 | convolution fusion | flops 4297064448 | bytes 13631488 | tf_op jit(solution)/shard_map/dot_general | solution.py:145
  393.7 48.4 %reduce-scatter.2.cloned.1.call-done = bf16[128,4096]{1,0:T(8,128)(2,1)} async-done(((bf16[512,4096]{1,0:T(8,128)(2,1)}), bf16[128,4096]{1,0:T(8,128)(2,1)}) %reduce-scatter.2.cloned.1.call-update) | async-done | bytes 1048592 | tf_op jit(solution)/shard_map/reduce_scatter | solution.py:144
  (78 shorter events, 28.0 us)
Async XLA Ops:
  6.5 59.1 %copy-start = (bf16[4096,256]{1,0:T(8,128)(2,1)S(1)}, bf16[4096,256]{1,0:T(8,128)(2,1)}, u32[]{:S(2)}) copy-start(bf16[4096,256]{1,0:T(8,128)(2,1)} %param.10) | copy-start | bytes 6291460
  6.5 53.9 %all-gather.3.cloned.1.call-start = ((), (), s32[]{:S(2)}) async-start(), calls=%async_computation.1 | async-start | bytes 5242880 | tf_op jit(solution)/shard_map/all_gather | solution.py:108
  7.3 314.3 %all-gather.5.cloned.1.call-start = ((), (), s32[]{:S(2)}) async-start(), calls=%async_computation.2 | async-start | bytes 8650752 | tf_op jit(solution)/shard_map/all_gather | solution.py:124
  7.9 56.8 %copy-start.6 = (f32[512,64]{0,1:T(8,128)}, f32[512,64]{0,1:T(8,128)S(1)}, u32[]{:S(2)}) copy-start(f32[512,64]{0,1:T(8,128)S(1)} %get-tuple-element.20) | copy-start | bytes 393220
  65.6 376.5 %reduce-scatter.2.cloned.1.call-start = ((), (), s32[]{:S(2)}) async-start(), calls=%async_computation.3 | async-start | bytes 5242880 | tf_op jit(solution)/shard_map/reduce_scatter | solution.py:144
  69.9 5.9 %collective-permute-start = (bf16[512,256]{1,0:T(8,128)(2,1)S(1)}, bf16[512,256]{1,0:T(8,128)(2,1)S(1)}, u32[]{:S(2)}, u32[]{:S(2)}) collective-permute-start(bf16[512,256]{1,0:T(8,128)(2,1)S(1)} %get-tuple-element.25), channel_id=1, source_target_pairs={{0,124},{4,0},{8,4},{12,8},{16,12},{20,16},{24,20},{28,24},{32,28}... | collective-permute-start | bytes 786440 | tf_op jit(solution)/shard_map/ppermute | solution.py:21
  75.8 19.3 %collective-permute-start.1 = (bf16[1024,256]{1,0:T(8,128)(2,1)S(1)}, bf16[1024,256]{1,0:T(8,128)(2,1)S(1)}, u32[]{:S(2)}, u32[]{:S(2)}) collective-permute-start(bf16[1024,256]{1,0:T(8,128)(2,1)S(1)} %pad_maximum_fusion.2), channel_id=1, source_target_pairs={{0,120},{4,124},{8,0},{12,4},{16,8},{20,12},{24,16},{28,20},{32,24... | collective-permute-start | bytes 1572872 | tf_op jit(solution)/shard_map/ppermute | solution.py:21
  95.2 41.5 %collective-permute-start.2 = (bf16[2048,256]{1,0:T(8,128)(2,1)S(1)}, bf16[2048,256]{1,0:T(8,128)(2,1)S(1)}, u32[]{:S(2)}, u32[]{:S(2)}) collective-permute-start(bf16[2048,256]{1,0:T(8,128)(2,1)S(1)} %pad_maximum_fusion.1), channel_id=1, source_target_pairs={{0,112},{4,116},{8,120},{12,124},{16,0},{20,4},{24,8},{28,12},{32,... | collective-permute-start | bytes 3145736 | tf_op jit(solution)/shard_map/ppermute | solution.py:21
  136.8 46.7 %collective-permute-start.3 = (bf16[4096,256]{1,0:T(8,128)(2,1)S(1)}, bf16[4096,256]{1,0:T(8,128)(2,1)S(1)}, u32[]{:S(2)}, u32[]{:S(2)}) collective-permute-start(bf16[4096,256]{1,0:T(8,128)(2,1)S(1)} %pad_maximum_fusion), channel_id=1, source_target_pairs={{0,96},{4,100},{8,104},{12,108},{16,112},{20,116},{24,120},{28,124... | collective-permute-start | bytes 6291464 | tf_op jit(solution)/shard_map/ppermute | solution.py:21
  138.8 48.4 %copy-start.9 = (s32[4,8]{1,0:T(4,128)S(1)}, s32[4,8]{1,0:T(4,128)}, u32[]{:S(2)}) copy-start(s32[4,8]{1,0:T(4,128)} %param.12) | copy-start | bytes 388
  138.8 48.5 %copy-start.10 = (s32[16]{0:T(128)S(1)}, s32[16]{0:T(128)}, u32[]{:S(2)}) copy-start(s32[16]{0:T(128)} %param.13) | copy-start | bytes 196
  183.5 1.4 copy-start.2
  187.2 94.0 %collective-permute-start.4 = (bf16[8192,256]{1,0:T(8,128)(2,1)}, bf16[8192,256]{1,0:T(8,128)(2,1)}, u32[]{:S(2)}, u32[]{:S(2)}) collective-permute-start(bf16[8192,256]{1,0:T(8,128)(2,1)} %get-tuple-element.7), channel_id=1, source_target_pairs={{0,64},{4,68},{8,72},{12,76},{16,80},{20,84},{24,88},{28,92},{32,9... | collective-permute-start | bytes 12582920 | tf_op jit(solution)/shard_map/ppermute | solution.py:21
  192.3 8.3 %copy-start.7 = (f32[512,64]{0,1:T(8,128)S(1)}, f32[512,64]{0,1:T(8,128)}, u32[]{:S(2)}) copy-start(f32[512,64]{0,1:T(8,128)} %copy-done.6) | copy-start | bytes 393220
  285.7 3.4 copy-start.3
  341.9 4.1 copy-start.4
  346.1 10.5 %copy-start.8 = (pred[4,128,1024]{1,2,0:T(8,128)(4,1)S(1)}, pred[4,128,1024]{1,2,0:T(8,128)(4,1)}, u32[]{:S(2)}) copy-start(pred[4,128,1024]{1,2,0:T(8,128)(4,1)} %and_and_fusion) | copy-start | bytes 1572868
  356.6 19.8 %copy-start.5 = (bf16[4,1024,2,128]{3,2,1,0:T(2,128)(2,1)S(1)}, bf16[4,1024,2,128]{3,2,1,0:T(2,128)(2,1)}, u32[]{:S(2)}) copy-start(bf16[4,1024,2,128]{3,2,1,0:T(2,128)(2,1)} %reshape.220) | copy-start | bytes 6291460
  384.1 58.0 %copy-start.1 = (bf16[4096,256]{1,0:T(8,128)(2,1)S(1)}, bf16[4096,256]{1,0:T(8,128)(2,1)}, u32[]{:S(2)}) copy-start(bf16[4096,256]{1,0:T(8,128)(2,1)} %param.10) | copy-start | bytes 6291460
Sparse Core Ops, SparseCore 0:
  9.0 51.3 all-gather.2
  65.8 75.1 all-gather.4
  393.8 48.2 reduce-scatter.1
